TPU v7x, 256 devices: a whole 4x4x8 slice. The times are simulated.
256 devices in a mesh: layer: 8 (over x, z_hi), latent: 8 (over z_lo, core), token: 4 (over y).
Axes of the slice: x: 4, y: 4, z: 8 (z_hi: 2, z_lo: 4; z = z_hi * 4 + z_lo), core: 2. Of those that a mesh axis runs over, the one named last changes fastest.
Arguments:
- streams: bfloat16 [8, 4096, 8192], P('layer', 'token', 'latent'), may hold values from -6 to 6
- active_latents: int32 [4096, 64], P('token'), may hold values from 0 to 383, all different within a row
- enc_weight: float32 [8, 384, 8192], P('layer', 'latent', 'token'), may hold values from -6 to 6
- enc_moment: float32 [8, 384, 8192], P('layer', 'latent', 'token'), may hold values from -0.0029296875 to 0.0029296875
- enc_second: float32 [8, 384, 8192], P('layer', 'latent', 'token'), may hold values from 1e-09 to 1e-07
- dec_weight: float32 [8, 384, 8192], P('layer', 'latent', 'token'), may hold values from -6 to 6
- dec_moment: float32 [8, 384, 8192], P('layer', 'latent', 'token'), may hold values from -0.0029296875 to 0.0029296875
- dec_second: float32 [8, 384, 8192], P('layer', 'latent', 'token'), may hold values from 1e-09 to 1e-07
Outputs:
- enc_weight_new: float32 [8, 384, 8192], P('layer', 'latent', 'token')
- enc_moment_new: float32 [8, 384, 8192], P('layer', 'latent', 'token')
- enc_second_new: float32 [8, 384, 8192], P('layer', 'latent', 'token')
- dec_weight_new: float32 [8, 384, 8192], P('layer', 'latent', 'token')
- dec_moment_new: float32 [8, 384, 8192], P('layer', 'latent', 'token')
- dec_second_new: float32 [8, 384, 8192], P('layer', 'latent', 'token')
Inputs may be any that keep to these rules, and one draw needn't show every extreme that they name: `active_latents`: each row names 64 different latents; every latent is named by some row.
All inputs are finite; a program needn't handle non-finite values.
Results may differ from a plain program's by a relative error of at most 0.0056.
Values may be sent and summed in bfloat16 or wider, within the bound.
No kernel may reach another device: no remote copies, remote signals or barrier semaphores. Data moves between devices by JAX's collectives and lax.ppermute only.
A program may use at most 64 MiB of HBM per device.

v0:
```python
import math
import jax
import jax.numpy as jnp
from jax import lax
from jax.sharding import PartitionSpec as P

K = 64
ADAM_STEP = 100


def adam_step(weight, moment, second, gradient):
    moment_new = 0.9 * moment + 0.1 * gradient
    second_new = 0.999 * second + 0.001 * gradient * gradient
    first_fix = 1.0 - 0.9**ADAM_STEP
    second_fix = 1.0 - 0.999**ADAM_STEP
    weight_new = weight - 0.2 * (moment_new / first_fix) / (
        jnp.sqrt(second_new / second_fix) + 1e-08
    )
    return (weight_new, moment_new, second_new)


def contract(left, right, left_dim, right_dim):
    return lax.dot_general(
        left, right, (((left_dim,), (right_dim,)), ((), ())), preferred_element_type=jnp.float32
    )


def matches(active_latents, total_lat):
    latent_ids = jnp.arange(total_lat, dtype=jnp.int32)[None, None, :]
    return active_latents[:, :, None] == latent_ids


def masked_total(partial_value, selected):
    summed = lax.psum(partial_value, ("layer", "latent"))
    return (summed * selected).astype(jnp.bfloat16)


def body(
    streams, active_latents, enc_weight, enc_moment, enc_second, dec_weight, dec_moment, dec_second
):
    tok_rows = streams.shape[1]
    lat_dev = enc_weight.shape[1]
    n_layer = lax.axis_size("layer")
    total_lat = lat_dev * lax.axis_size("latent")
    features = enc_weight.shape[2] * lax.axis_size("token")
    tokens_all = tok_rows * lax.axis_size("token")
    enc_scale = 1.0 / math.sqrt(n_layer * features)
    dec_scale = 1.0 / math.sqrt(K)
    casted = (enc_weight[0].astype(jnp.bfloat16), dec_weight[0].astype(jnp.bfloat16))
    gathered = (
        lax.all_gather(casted[0], "token", axis=1, tiled=True),
        lax.all_gather(casted[1], "token", axis=1, tiled=True),
    )
    enc_cols, dec_cols = (
        lax.all_to_all(gathered[0], "latent", split_axis=1, concat_axis=0, tiled=True),
        lax.all_to_all(gathered[1], "latent", split_axis=1, concat_axis=0, tiled=True),
    )
    own_rows = streams[0]
    selected = jnp.sum(matches(active_latents, total_lat).astype(jnp.float32), axis=1)
    pre_partial = contract(own_rows, enc_cols, 1, 1) * enc_scale
    latent_codes = masked_total(pre_partial, selected)
    rebuilt = jnp.dot(latent_codes, dec_cols, preferred_element_type=jnp.float32) * dec_scale
    errors = (rebuilt - own_rows.astype(jnp.float32)).astype(jnp.bfloat16)
    back_partial = contract(errors, dec_cols, 1, 1) * dec_scale
    backward = masked_total(back_partial, selected)
    dec_partial = contract(latent_codes, errors, 0, 0) * (dec_scale / tokens_all)
    enc_partial = contract(backward, own_rows, 0, 0) * (enc_scale / tokens_all)
    exchanged = (
        lax.all_to_all(enc_partial, "latent", split_axis=0, concat_axis=1, tiled=True),
        lax.all_to_all(dec_partial, "latent", split_axis=0, concat_axis=1, tiled=True),
    )
    enc_grad, dec_grad = (
        lax.psum_scatter(exchanged[0], "token", scatter_dimension=1, tiled=True),
        lax.psum_scatter(exchanged[1], "token", scatter_dimension=1, tiled=True),
    )
    enc_out = adam_step(enc_weight[0], enc_moment[0], enc_second[0], enc_grad)
    dec_out = adam_step(dec_weight[0], dec_moment[0], dec_second[0], dec_grad)
    return (
        enc_out[0][None],
        enc_out[1][None],
        enc_out[2][None],
        dec_out[0][None],
        dec_out[1][None],
        dec_out[2][None],
    )


def solution(mesh):
    in_specs = (
        P("layer", "token", "latent"),
        P("token", None),
        P("layer", "latent", "token"),
        P("layer", "latent", "token"),
        P("layer", "latent", "token"),
        P("layer", "latent", "token"),
        P("layer", "latent", "token"),
        P("layer", "latent", "token"),
    )
    out_specs = (
        P("layer", "latent", "token"),
        P("layer", "latent", "token"),
        P("layer", "latent", "token"),
        P("layer", "latent", "token"),
        P("layer", "latent", "token"),
        P("layer", "latent", "token"),
    )
    return jax.shard_map(body, mesh=mesh, in_specs=in_specs, out_specs=out_specs, check_vma=False)
```

profile of v0, /device:TPU:2, one launch (start us, length us, event | category | flops | bytes accessed | tf_op | source)
XLA Modules:
  0.0 534.7 jit_solution(17642249158765734346)
XLA Ops:
  7.2 1.0 bitcast_convert_fusion.1
  8.2 13.8 %all_gather.6 = bf16[48,8192]{1,0:T(8,128)(2,1)S(1)} all-gather(bf16[48,2048]{1,0:T(8,128)(2,1)S(1)} %bitcast_convert_fusion.1), channel_id=1, replica_groups=mesh['layer'=8,'latent'=8,'token'=4] {'token'}, dimensions={1}, use_global_device_ids=true | all-gather | bytes 983040 | tf_op jit(solution)/shard_map/all_gather | solution.py:51
  23.0 6.0 %all-to-all-start = ((bf16[48,8,1024]{2,0,1:T(8,128)(2,1)}), bf16[48,8,1024]{2,0,1:T(8,128)(2,1)}, u32[]{:S(2)}, u32[]{:S(2)}) async-start(bf16[48,8,1024]{2,0,1:T(8,128)(2,1)} %bitcast.84), calls=%async_computation | async-start | bytes 1572864 | tf_op jit(solution)/shard_map/all_to_all | solution.py:55
  29.3 14.4 %all_gather.7 = bf16[48,8192]{1,0:T(8,128)(2,1)S(1)} all-gather(bf16[48,2048]{1,0:T(8,128)(2,1)S(1)} %bitcast_convert_fusion), channel_id=1, replica_groups=mesh['layer'=8,'latent'=8,'token'=4] {'token'}, dimensions={1}, use_global_device_ids=true | all-gather | bytes 983040 | tf_op jit(solution)/shard_map/all_gather | solution.py:52
  43.7 1.0 copy.41
  44.7 5.4 %all-to-all-done = bf16[48,8,1024]{2,0,1:T(8,128)(2,1)} async-done(((bf16[48,8,1024]{2,0,1:T(8,128)(2,1)}), bf16[48,8,1024]{2,0,1:T(8,128)(2,1)}, u32[]{:S(2)}, u32[]{:S(2)}) %all-to-all-start) | async-done | bytes 786464 | tf_op jit(solution)/shard_map/all_to_all | solution.py:55
  50.1 4.2 all-to-all-start.1
  54.4 3.5 fusion.4
  58.0 17.8 %convert_reduce_fusion = f32[1024,384]{1,0:T(8,128)S(1)} fusion(s32[1024,64]{1,0:T(8,128)S(1)} %copy.31), kind=kLoop, calls=%fused_computation | loop fusion | flops 75104256 | bytes 1835008 | tf_op jit(solution)/shard_map/reduce_sum | solution.py:59
  75.8 172.1 %all-reduce.3.cloned.1.call-done = f32[1024,384]{1,0:T(8,128)} async-done(((f32[1024,384]{1,0:T(8,128)}), f32[1024,384]{1,0:T(8,128)}) %all-reduce.3.cloned.1.call-update) | async-done | bytes 1572880 | tf_op jit(solution)/shard_map/psum | solution.py:34
  247.8 1.6 multiply_convert_fusion.1
  249.4 3.1 subtract_convert_fusion
  252.5 2.1 convolution_multiply_fusion
  254.7 3.6 all-to-all-start.3
  258.3 4.2 convolution_multiply_fusion.1
  262.6 35.6 %all-to-all-done.3 = f32[8,48,1024]{2,1,0:T(8,128)S(1)} async-done(((f32[8,48,1024]{2,1,0:T(8,128)}), f32[8,48,1024]{2,1,0:T(8,128)S(1)}, u32[]{:S(2)}, u32[]{:S(2)}) %all-to-all-start.3) | async-done | bytes 1572896 | tf_op jit(solution)/shard_map/all_to_all | solution.py:70
  298.2 1.2 copy.38
  299.5 154.2 %all-reduce.5.cloned.1.call-done = f32[1024,384]{1,0:T(8,128)} async-done(((f32[1024,384]{1,0:T(8,128)}), f32[1024,384]{1,0:T(8,128)}) %all-reduce.5.cloned.1.call-update) | async-done | bytes 1572880 | tf_op jit(solution)/shard_map/psum | solution.py:34
  453.8 3.1 fusion.7
  456.8 40.9 %all_to_all.76 = f32[8,48,1024]{2,1,0:T(8,128)S(1)} all-to-all(f32[8,48,1024]{2,1,0:T(8,128)S(1)} %bitcast.90), channel_id=1, replica_groups=mesh['layer'=8,'latent'=8,'token'=4] {'latent'}, dimensions={0} | all-to-all | bytes 3145728 | tf_op jit(solution)/shard_map/all_to_all | solution.py:69
  497.7 1.3 copy.37
  500.2 2.2 fusion.16
  502.4 23.5 %reduce-scatter.3.cloned.1.call-done = f32[48,2048]{1,0:T(8,128)} async-done(((f32[48,8192]{1,0:T(8,128)}), f32[48,2048]{1,0:T(8,128)}) %reduce-scatter.3.cloned.1.call-update) | async-done | bytes 393232 | tf_op jit(solution)/shard_map/reduce_scatter | solution.py:73
  525.9 2.3 fusion.17
  (31 shorter events, 2.5 us)
Async XLA Ops:
  22.0 7.0 %copy-start.8 = (s32[1024,64]{0,1:T(8,128)S(1)}, s32[1024,64]{0,1:T(8,128)}, u32[]{:S(2)}) copy-start(s32[1024,64]{0,1:T(8,128)} %param.9) | copy-start | bytes 786436
  23.0 6.2 %copy-start.2 = (f32[1,48,2048]{2,1,0:T(8,128)S(1)}, f32[1,48,2048]{2,1,0:T(8,128)}, u32[]{:S(2)}) copy-start(f32[1,48,2048]{2,1,0:T(8,128)} %param.13) | copy-start | bytes 1179652
  23.0 27.1 %all-to-all-start = ((bf16[48,8,1024]{2,0,1:T(8,128)(2,1)}), bf16[48,8,1024]{2,0,1:T(8,128)(2,1)}, u32[]{:S(2)}, u32[]{:S(2)}) async-start(bf16[48,8,1024]{2,0,1:T(8,128)(2,1)} %bitcast.84), calls=%async_computation | async-start | bytes 1572864 | tf_op jit(solution)/shard_map/all_to_all | solution.py:55
  43.7 10.7 %copy-start = (bf16[1,1024,1024]{2,1,0:T(8,128)(2,1)S(1)}, bf16[1,1024,1024]{2,1,0:T(8,128)(2,1)}, u32[]{:S(2)}) copy-start(bf16[1,1024,1024]{2,1,0:T(8,128)(2,1)} %param.8) | copy-start | bytes 6291460
  50.1 199.3 %all-to-all-start.1 = ((bf16[48,8,1024]{2,0,1:T(8,128)(2,1)}), bf16[48,8,1024]{2,0,1:T(8,128)(2,1)}, u32[]{:S(2)}, u32[]{:S(2)}) async-start(bf16[48,8,1024]{2,0,1:T(8,128)(2,1)} %bitcast.83), calls=%async_computation.1 | async-start | bytes 1572864 | tf_op jit(solution)/shard_map/all_to_all | solution.py:56
  54.3 193.5 %all-reduce.3.cloned.1.call-start = ((), (), s32[]{:S(2)}) async-start(), calls=%async_computation.6 | async-start | bytes 3145728 | tf_op jit(solution)/shard_map/psum | solution.py:34
  252.5 2.2 copy-start.1
  254.7 43.6 %all-to-all-start.3 = ((f32[8,48,1024]{2,1,0:T(8,128)}), f32[8,48,1024]{2,1,0:T(8,128)S(1)}, u32[]{:S(2)}, u32[]{:S(2)}) async-start(f32[8,48,1024]{2,1,0:T(8,128)} %bitcast.87), calls=%async_computation.4 | async-start | bytes 3145728 | tf_op jit(solution)/shard_map/all_to_all | solution.py:70
  258.2 195.5 %all-reduce.5.cloned.1.call-start = ((), (), s32[]{:S(2)}) async-start(), calls=%async_computation.7 | async-start | bytes 3145728 | tf_op jit(solution)/shard_map/psum | solution.py:34
  262.5 236.6 %reduce-scatter.5.cloned.1.call-start = ((), (), s32[]{:S(2)}) async-start(), calls=%async_computation.9 | async-start | bytes 1966080 | tf_op jit(solution)/shard_map/reduce_scatter | solution.py:74
  299.5 226.4 %reduce-scatter.3.cloned.1.call-start = ((), (), s32[]{:S(2)}) async-start(), calls=%async_computation.8 | async-start | bytes 1966080 | tf_op jit(solution)/shard_map/reduce_scatter | solution.py:73
  499.0 1.0 copy-start.4
  499.0 1.1 copy-start.5
  499.1 26.9 %copy-start.3 = (f32[1,48,2048]{2,1,0:T(8,128)S(1)}, f32[1,48,2048]{2,1,0:T(8,128)}, u32[]{:S(2)}) copy-start(f32[1,48,2048]{2,1,0:T(8,128)} %param.10) | copy-start | bytes 1179652
  499.1 26.8 %copy-start.6 = (f32[1,48,2048]{2,1,0:T(8,128)S(1)}, f32[1,48,2048]{2,1,0:T(8,128)}, u32[]{:S(2)}) copy-start(f32[1,48,2048]{2,1,0:T(8,128)} %param.12) | copy-start | bytes 1179652
  499.1 26.8 %copy-start.7 = (f32[1,48,2048]{2,1,0:T(8,128)S(1)}, f32[1,48,2048]{2,1,0:T(8,128)}, u32[]{:S(2)}) copy-start(f32[1,48,2048]{2,1,0:T(8,128)} %param.11) | copy-start | bytes 1179652
Sparse Core Ops, SparseCore 0:
  58.6 189.2 all-reduce.2
  262.7 191.0 all-reduce.4
  456.3 27.2 reduce-scatter.4
  499.2 26.6 reduce-scatter.2
where the time goes:
time: 535 us
  waiting for transfers between devices  391 us (73%)
  blocking collectives  69.1 us (13%)
  other arithmetic  24.9 us (5%)
  matrix products  16.1 us (3%)
  starting transfers between devices  14 us (3%)
  between operations  13.9 us (3%)
  local copies, waits for them, and re-layouts  5.76 us (1%)
    psum x2, waiting for transfers between devices, masked_total(): summed = lax.psum(partial_value, ('layer', 'latent'))  326 us
    all_to_all x1, blocking collectives, body(): lax.all_to_all(enc_partial, 'latent', split_axis=0, concat_axis=1, tiled=...  40.9 us
    all_to_all x1, waiting for transfers between devices, body(): lax.all_to_all(dec_partial, 'latent', split_axis=0, concat_axis=1, tiled=...  35.6 us
    reduce_scatter x1, waiting for transfers between devices, body(): lax.psum_scatter(exchanged[0], 'token', scatter_dimension=1, tiled=True)  23.5 us
    reduce_sum x1, other arithmetic, body(): jnp.sum(matches(active_latents, total_lat).astype(jnp.float32), axis=1)  17.8 us
    all_gather x1, blocking collectives, body(): lax.all_gather(casted[1], 'token', axis=1, tiled=True)  14.4 us
    all_gather x1, blocking collectives, body(): lax.all_gather(casted[0], 'token', axis=1, tiled=True)  13.8 us
    dot_general x4, matrix products, contract(): lax.dot_general(left, right, (((left_dim,), (right_dim,)), ((), ())), pre...  13 us
  transfers between devices with their start and end apart: 7, of which 5 were waited for; matrix products, arithmetic and copies ran while one was open for 7% of the time, Pallas kernels for 0%

commit v1 on v0

--- a/solution.py
+++ b/solution.py
@@ -65,9 +65,19 @@
     backward = masked_total(back_partial, selected)
     dec_partial = contract(latent_codes, errors, 0, 0) * (dec_scale / tokens_all)
     enc_partial = contract(backward, own_rows, 0, 0) * (enc_scale / tokens_all)
+
+    def answer_sectors(s0, which_axis):
+        val2 = jax.lax.all_to_all(
+            jnp.stack(jnp.split(s0, jax.lax.axis_size(which_axis), axis=0)),
+            which_axis,
+            split_axis=0,
+            concat_axis=0,
+        )
+        return jnp.concatenate(val2, axis=1)
+
     exchanged = (
         lax.all_to_all(enc_partial, "latent", split_axis=0, concat_axis=1, tiled=True),
-        lax.all_to_all(dec_partial, "latent", split_axis=0, concat_axis=1, tiled=True),
+        answer_sectors(dec_partial, "latent"),
     )
     enc_grad, dec_grad = (
         lax.psum_scatter(exchanged[0], "token", scatter_dimension=1, tiled=True),

time: 535 us -> 540 us (level)
  local copies, waits for them, and re-layouts: 5.76 us -> 11.6 us
where the time goes in v1:
time: 540 us; the launch traced here: 539 us
  waiting for transfers between devices  391 us (72%)
  blocking collectives  69.1 us (13%)
  other arithmetic  24.9 us (5%)
  matrix products  14.9 us (3%)
  starting transfers between devices  14 us (3%)
  between operations  13.9 us (3%)
  local copies, waits for them, and re-layouts  11.6 us (2%)
    psum x2, waiting for transfers between devices, masked_total(): summed = lax.psum(partial_value, ('layer', 'latent'))  326 us
    all_to_all x1, blocking collectives, body(): lax.all_to_all(enc_partial, 'latent', split_axis=0, concat_axis=1, tiled=...  40.9 us
    all_to_all x1, waiting for transfers between devices, answer_sectors(): jax.lax.all_to_all(jnp.stack(jnp.split(s0, jax.lax.axis_size(which_axis),...  35.7 us
    reduce_scatter x1, waiting for transfers between devices, body(): lax.psum_scatter(exchanged[0], 'token', scatter_dimension=1, tiled=True)  23.5 us
    reduce_sum x1, other arithmetic, body(): jnp.sum(matches(active_latents, total_lat).astype(jnp.float32), axis=1)  17.8 us
    all_gather x1, blocking collectives, body(): lax.all_gather(casted[1], 'token', axis=1, tiled=True)  14.4 us
    all_gather x1, blocking collectives, body(): lax.all_gather(casted[0], 'token', axis=1, tiled=True)  13.8 us
    dot_general x4, matrix products, contract(): lax.dot_general(left, right, (((left_dim,), (right_dim,)), ((), ())), pre...  11.8 us
  transfers between devices with their start and end apart: 7, of which 5 were waited for; matrix products, arithmetic and copies ran while one was open for 7% of the time, Pallas kernels for 0%

profile of v1, /device:TPU:2, one launch (start us, length us, event | category | flops | bytes accessed | tf_op | source)
XLA Modules:
  0.0 539.4 jit_solution(18031079360154215731)
XLA Ops:
  7.2 1.0 bitcast_convert_fusion.1
  8.2 13.8 %all_gather.6 = bf16[48,8192]{1,0:T(8,128)(2,1)S(1)} all-gather(bf16[48,2048]{1,0:T(8,128)(2,1)S(1)} %bitcast_convert_fusion.1), channel_id=1, replica_groups=mesh['layer'=8,'latent'=8,'token'=4] {'token'}, dimensions={1}, use_global_device_ids=true | all-gather | bytes 983040 | tf_op jit(solution)/shard_map/all_gather | solution.py:51
  23.0 6.0 %all-to-all-start = ((bf16[48,8,1024]{2,0,1:T(8,128)(2,1)}), bf16[48,8,1024]{2,0,1:T(8,128)(2,1)}, u32[]{:S(2)}, u32[]{:S(2)}) async-start(bf16[48,8,1024]{2,0,1:T(8,128)(2,1)} %bitcast.115), calls=%async_computation | async-start | bytes 1572864 | tf_op jit(solution)/shard_map/all_to_all | solution.py:55
  29.3 14.4 %all_gather.7 = bf16[48,8192]{1,0:T(8,128)(2,1)S(1)} all-gather(bf16[48,2048]{1,0:T(8,128)(2,1)S(1)} %bitcast_convert_fusion), channel_id=1, replica_groups=mesh['layer'=8,'latent'=8,'token'=4] {'token'}, dimensions={1}, use_global_device_ids=true | all-gather | bytes 983040 | tf_op jit(solution)/shard_map/all_gather | solution.py:52
  43.7 1.0 copy.40
  44.7 5.4 %all-to-all-done = bf16[48,8,1024]{2,0,1:T(8,128)(2,1)} async-done(((bf16[48,8,1024]{2,0,1:T(8,128)(2,1)}), bf16[48,8,1024]{2,0,1:T(8,128)(2,1)}, u32[]{:S(2)}, u32[]{:S(2)}) %all-to-all-start) | async-done | bytes 786464 | tf_op jit(solution)/shard_map/all_to_all | solution.py:55
  50.1 4.2 all-to-all-start.1
  54.4 3.5 fusion.4
  58.0 17.8 %convert_reduce_fusion = f32[1024,384]{1,0:T(8,128)S(1)} fusion(s32[1024,64]{1,0:T(8,128)S(1)} %copy.30), kind=kLoop, calls=%fused_computation | loop fusion | flops 75104256 | bytes 1835008 | tf_op jit(solution)/shard_map/reduce_sum | solution.py:59
  75.8 172.1 %all-reduce.3.cloned.1.call-done = f32[1024,384]{1,0:T(8,128)} async-done(((f32[1024,384]{1,0:T(8,128)}), f32[1024,384]{1,0:T(8,128)}) %all-reduce.3.cloned.1.call-update) | async-done | bytes 1572880 | tf_op jit(solution)/shard_map/psum | solution.py:34
  247.8 1.6 multiply_convert_fusion.1
  249.4 3.1 subtract_convert_fusion
  252.5 1.0 convolution_multiply_fusion
  259.3 3.6 all-to-all-start.3
  263.0 4.2 convolution_multiply_fusion.1
  267.3 35.7 %all-to-all-done.3 = f32[8,48,1024]{2,1,0:T(8,128)S(1)} async-done(((f32[8,48,1024]{2,1,0:T(8,128)}), f32[8,48,1024]{2,1,0:T(8,128)S(1)}, u32[]{:S(2)}, u32[]{:S(2)}) %all-to-all-start.3) | async-done | bytes 1572896 | tf_op jit(solution)/shard_map/all_to_all | solution.py:70
  302.9 1.3 copy.37
  304.3 154.2 %all-reduce.5.cloned.1.call-done = f32[1024,384]{1,0:T(8,128)} async-done(((f32[1024,384]{1,0:T(8,128)}), f32[1024,384]{1,0:T(8,128)}) %all-reduce.5.cloned.1.call-update) | async-done | bytes 1572880 | tf_op jit(solution)/shard_map/psum | solution.py:34
  458.5 3.1 fusion.7
  461.5 40.9 %all_to_all.62 = f32[8,48,1024]{2,1,0:T(8,128)S(1)} all-to-all(f32[8,48,1024]{2,1,0:T(8,128)S(1)} %bitcast.120), channel_id=1, replica_groups=mesh['layer'=8,'latent'=8,'token'=4] {'latent'}, dimensions={0} | all-to-all | bytes 3145728 | tf_op jit(solution)/shard_map/all_to_all | solution.py:79
  502.4 1.3 copy.36
  504.8 2.2 fusion.24
  507.1 23.5 %reduce-scatter.3.cloned.1.call-done = f32[48,2048]{1,0:T(8,128)} async-done(((f32[48,8192]{1,0:T(8,128)}), f32[48,2048]{1,0:T(8,128)}) %reduce-scatter.3.cloned.1.call-update) | async-done | bytes 393232 | tf_op jit(solution)/shard_map/reduce_scatter | solution.py:83
  530.6 2.3 fusion.25
  (39 shorter events, 8.3 us)
Async XLA Ops:
  22.0 7.0 %copy-start.8 = (s32[1024,64]{0,1:T(8,128)S(1)}, s32[1024,64]{0,1:T(8,128)}, u32[]{:S(2)}) copy-start(s32[1024,64]{0,1:T(8,128)} %param.9) | copy-start | bytes 786436
  23.0 6.2 %copy-start.2 = (f32[1,48,2048]{2,1,0:T(8,128)S(1)}, f32[1,48,2048]{2,1,0:T(8,128)}, u32[]{:S(2)}) copy-start(f32[1,48,2048]{2,1,0:T(8,128)} %param.13) | copy-start | bytes 1179652
  23.0 27.1 %all-to-all-start = ((bf16[48,8,1024]{2,0,1:T(8,128)(2,1)}), bf16[48,8,1024]{2,0,1:T(8,128)(2,1)}, u32[]{:S(2)}, u32[]{:S(2)}) async-start(bf16[48,8,1024]{2,0,1:T(8,128)(2,1)} %bitcast.115), calls=%async_computation | async-start | bytes 1572864 | tf_op jit(solution)/shard_map/all_to_all | solution.py:55
  43.7 10.7 %copy-start = (bf16[1,1024,1024]{2,1,0:T(8,128)(2,1)S(1)}, bf16[1,1024,1024]{2,1,0:T(8,128)(2,1)}, u32[]{:S(2)}) copy-start(bf16[1,1024,1024]{2,1,0:T(8,128)(2,1)} %param.8) | copy-start | bytes 6291460
  50.1 199.3 %all-to-all-start.1 = ((bf16[48,8,1024]{2,0,1:T(8,128)(2,1)}), bf16[48,8,1024]{2,0,1:T(8,128)(2,1)}, u32[]{:S(2)}, u32[]{:S(2)}) async-start(bf16[48,8,1024]{2,0,1:T(8,128)(2,1)} %bitcast.114), calls=%async_computation.1 | async-start | bytes 1572864 | tf_op jit(solution)/shard_map/all_to_all | solution.py:56
  54.3 193.5 %all-reduce.3.cloned.1.call-start = ((), (), s32[]{:S(2)}) async-start(), calls=%async_computation.6 | async-start | bytes 3145728 | tf_op jit(solution)/shard_map/psum | solution.py:34
  252.5 1.3 copy-start.1
  259.3 43.6 %all-to-all-start.3 = ((f32[8,48,1024]{2,1,0:T(8,128)}), f32[8,48,1024]{2,1,0:T(8,128)S(1)}, u32[]{:S(2)}, u32[]{:S(2)}) async-start(f32[8,48,1024]{2,1,0:T(8,128)} %fusion.14), calls=%async_computation.4 | async-start | bytes 3145728 | tf_op jit(solution)/shard_map/all_to_all | solution.py:70
  262.9 195.5 %all-reduce.5.cloned.1.call-start = ((), (), s32[]{:S(2)}) async-start(), calls=%async_computation.7 | async-start | bytes 3145728 | tf_op jit(solution)/shard_map/psum | solution.py:34
  267.2 236.6 %reduce-scatter.5.cloned.1.call-start = ((), (), s32[]{:S(2)}) async-start(), calls=%async_computation.9 | async-start | bytes 1966080 | tf_op jit(solution)/shard_map/reduce_scatter | solution.py:84
  304.2 226.3 %reduce-scatter.3.cloned.1.call-start = ((), (), s32[]{:S(2)}) async-start(), calls=%async_computation.8 | async-start | bytes 1966080 | tf_op jit(solution)/shard_map/reduce_scatter | solution.py:83
  503.7 1.0 copy-start.4
  503.7 1.1 copy-start.5
  503.7 26.9 %copy-start.3 = (f32[1,48,2048]{2,1,0:T(8,128)S(1)}, f32[1,48,2048]{2,1,0:T(8,128)}, u32[]{:S(2)}) copy-start(f32[1,48,2048]{2,1,0:T(8,128)} %param.10) | copy-start | bytes 1179652
  503.7 26.8 %copy-start.6 = (f32[1,48,2048]{2,1,0:T(8,128)S(1)}, f32[1,48,2048]{2,1,0:T(8,128)}, u32[]{:S(2)}) copy-start(f32[1,48,2048]{2,1,0:T(8,128)} %param.12) | copy-start | bytes 1179652
  503.8 26.8 %copy-start.7 = (f32[1,48,2048]{2,1,0:T(8,128)S(1)}, f32[1,48,2048]{2,1,0:T(8,128)}, u32[]{:S(2)}) copy-start(f32[1,48,2048]{2,1,0:T(8,128)} %param.11) | copy-start | bytes 1179652
Sparse Core Ops, SparseCore 0:
  58.6 189.2 all-reduce.2
  267.3 191.0 all-reduce.4
  461.0 27.2 reduce-scatter.4
  503.8 26.6 reduce-scatter.2
